TPU v7x, 32 devices: a whole 2x2x4 slice. The times are simulated.
32 devices in a mesh: rows: 4 (over y, x), past: 8 (over z, core).
Axes of the slice: x: 2, y: 2, z: 4, core: 2. Of those that a mesh axis runs over, the one named last changes fastest.
Arguments:
- tile_left: float32 [4, 8, 1024, 128], P('rows', 'past'), may hold values from -0.1875 to 0.1875
- tile_right: float32 [4, 8, 1024, 128], P('rows', 'past'), may hold values from -0.1875 to 0.1875
- diag_left: float32 [8, 1024, 128], P('past', 'rows'), may hold values from -6 to 6
- diag_right: float32 [8, 1024, 128], P('past', 'rows'), may hold values from -0.1875 to 0.1875
- present: int32 [4, 8], P('rows', 'past'), may hold values 0 or 1
- old_left: float32 [4, 1024, 128], P('rows'), may hold values from -6 to 6
- old_right: float32 [4, 1024, 128], P('rows'), may hold values from -0.1875 to 0.1875
- start: float32 [4, 1024, 128], P('rows'), may hold values from -6 to 6
Outputs:
- left: float32 [4, 1024, 128], P('rows')
- right: float32 [4, 1024, 128], P('rows')
Inputs may be any that keep to these rules, and one draw needn't show every extreme that they name: present is 1 exactly where the past tile of that tile row and panel is listed.
All inputs are finite; a program needn't handle non-finite values. No bound on the sum of `present` on one device may be relied on, other than what follows from the above.
Results may differ from a plain program's by a relative error of at most 0.00026.
Values sent between devices are 32-bit elements; how exact they have to be, the bound alone decides.
A program may use at most 64 MiB of HBM per device.

v0:
```python
import functools
import math

import jax
import jax.numpy as jnp
from jax import lax
from jax.experimental import pallas as pl
from jax.experimental.pallas import tpu as pltpu
from jax.sharding import PartitionSpec as P

ITERS = 3
HIGH = lax.Precision.HIGHEST
F32 = jnp.float32
BF16 = jnp.bfloat16
MESH = pl.DeviceIdType.MESH
NN = (((1,), (0,)), ((), ()))
NT = (((1,), (1,)), ((), ()))
TN = (((0,), (0,)), ((), ()))


def halves(value):
    high = value.astype(BF16)
    return high, (value - high.astype(F32)).astype(BF16)


def dot(left, right, dims, precision=None):
    return lax.dot_general(left, right, dims, precision=precision, preferred_element_type=F32)


def wide_nt(left, right):
    lh, ll = halves(left)
    rh, rl = halves(right)
    return dot(jnp.concatenate([lh, lh, ll], 1), jnp.concatenate([rh, rl, rh], 1), NT)


def lower_inverse(gram):
    size = gram.shape[0]
    rows = [gram[8 * b : 8 * b + 8] for b in range(size // 8)]
    lane = lax.broadcasted_iota(jnp.int32, (8, size), 1)
    sub = lax.broadcasted_iota(jnp.int32, (8, size), 0)
    for k in range(size):
        own, s = divmod(k, 8)
        pivot_row = rows[own][s : s + 1]
        inverse = 1.0 / pivot_row[:, k : k + 1]
        at_pivot = lane == k
        scaled = jnp.broadcast_to(
            jnp.where(lane[:1] == k, 1.0, pivot_row) * inverse, (8, size)
        )
        for b in range(own, size // 8):
            if b == own and s == 7:
                continue
            factor = jnp.broadcast_to(rows[b][:, k : k + 1], (8, size))
            fresh = jnp.where(at_pivot, 0.0, rows[b]) - factor * scaled
            rows[b] = jnp.where(sub > s, fresh, rows[b]) if b == own else fresh
    out = []
    for b in range(size // 8):
        diagonal = lane == sub + 8 * b
        pivot = jnp.sum(jnp.where(diagonal, rows[b], 0.0), axis=1, keepdims=True)
        unit = jnp.where(lane < sub + 8 * b, rows[b], jnp.where(diagonal, 1.0, 0.0))
        out.append(unit * lax.rsqrt(pivot))
    return jnp.concatenate(out, 0)


def split_into(total_ref, high_ref, low_ref, index):
    order = total_ref.shape[0]
    tile = 128

    def body(t, carry):
        at = pl.ds(pl.multiple_of(t * tile, tile), tile)
        high, low = halves(total_ref[at, :])
        high_ref[index, at, :] = high
        low_ref[index, at, :] = low
        return carry

    lax.fori_loop(0, order // tile, body, 0)


def apply_matrix(high_ref, low_ref, index, block, out_ref):
    order, width = block.shape
    bh, bl = halves(block)
    both = jnp.concatenate([bh, bl], 1)
    tile = 256

    def body(t, carry):
        at = pl.ds(pl.multiple_of(t * tile, tile), tile)
        first = dot(high_ref[index, at, :], both, NN)
        second = dot(low_ref[index, at, :], bh, NN)
        out_ref[at, :] = first[:, :width] + (first[:, width:] + second)
        return carry

    lax.fori_loop(0, order // tile, body, 0)


def iterate(high_ref, low_ref, block_ref, left_ref, right_ref):
    order, width = block_ref.shape

    def step(t, carry):
        apply_matrix(high_ref, low_ref, lax.rem(t, 2), block_ref[...], right_ref)
        value = right_ref[...]
        inverse = lower_inverse(dot(value, value, TN, HIGH))
        block_ref[...] = dot(value, inverse, NT, HIGH)
        return carry

    lax.fori_loop(0, 2 * ITERS + 1, step, 0)
    left_ref[...] = block_ref[...] * math.sqrt(order)
    apply_matrix(high_ref, low_ref, 1, block_ref[...], right_ref)


def accumulate(total_ref, left_ref, right_ref, first):
    order = left_ref.shape[0]
    tile = 256
    for index, (one, other) in enumerate(((left_ref, right_ref), (right_ref, left_ref))):
        oh, ol = halves(other[...])
        wide = jnp.concatenate([oh, ol, oh], 1)

        def body(t, carry):
            at = pl.ds(pl.multiple_of(t * tile, tile), tile)
            high, low = halves(one[at, :])
            value = dot(jnp.concatenate([high, high, low], 1), wide, NT)
            total_ref[index, at, :] = value if first else total_ref[index, at, :] - value
            return carry

        lax.fori_loop(0, order // tile, body, 0)


def gather_kernel(
    rows, past, tile_left, tile_right, diag_left, diag_right, weight, old_left, old_right, high, low,
    pbuf, dbuf, full, total,
    s_full, r_full, s_zd, r_zd, s_zp, r_zp, s_xd, r_xd, s_cp, r_cp, s_cd, r_cd,
):
    row = lax.axis_index("rows")
    me = lax.axis_index("past")
    core = lax.rem(me, 2)
    chip = me // 2
    chips = past // 2
    partner = me + 1 - 2 * core
    depth = diag_left.shape[0]
    peers = range(1, rows)

    def peer(d):
        return {"rows": lax.rem(row + d, rows), "past": me}

    def column(p):
        return {"rows": row, "past": p}

    barrier = pltpu.get_barrier_semaphore()
    for d in peers:
        pl.semaphore_signal(barrier, inc=1, device_id=peer(d), device_id_type=MESH)
    pl.semaphore_signal(barrier, inc=1, device_id=column(partner), device_id_type=MESH)

    @pl.when(chip > 0)
    def _():
        pl.semaphore_signal(barrier, inc=1, device_id=column(me - 2), device_id_type=MESH)

    @pl.when(chip < chips - 1)
    def _():
        pl.semaphore_signal(barrier, inc=1, device_id=column(me + 2), device_id_type=MESH)

    edge = jnp.logical_or(chip == 0, chip == chips - 1)

    @pl.when(edge)
    def _():
        pl.semaphore_wait(barrier, rows + min(chips - 1, 1))

    @pl.when(jnp.logical_not(edge))
    def _():
        pl.semaphore_wait(barrier, rows + 2)

    def send(src, dst, send_sem, recv_sem, device):
        return pltpu.make_async_remote_copy(
            src_ref=src, dst_ref=dst, send_sem=send_sem, recv_sem=recv_sem, device_id=device, device_id_type=MESH
        )

    def part(r):
        return pl.ds(pl.multiple_of(r * depth, depth), depth)

    def panel(src):
        return 2 * src + core

    def z_diag(src, way, own):
        piece = dbuf.at[panel(src), part(row)]
        return send(diag_left if own else piece, piece, s_zd.at[src, way], r_zd.at[src], column(me + 4 * way - 2))

    def z_tile(src, way):
        piece = pbuf.at[panel(src)]
        return send(piece, piece, s_zp.at[src, way], r_zp.at[src], column(me + 4 * way - 2))

    def x_diag(src, d, own):
        piece = dbuf.at[panel(src), part(row)]
        return send(diag_left if own else piece, piece, s_xd.at[src, d - 1], r_xd.at[src, d - 1], peer(d))

    def x_arrived(src, d):
        piece = dbuf.at[panel(src), part(lax.rem(row + rows - d, rows))]
        return send(piece, piece, s_xd.at[src, d - 1], r_xd.at[src, d - 1], peer(d))

    def c_tile(src, index):
        piece = pbuf.at[index]
        return send(piece, piece, s_cp.at[src], r_cp.at[src], column(partner))

    def c_diag(src, index):
        piece = dbuf.at[index]
        return send(piece, piece, s_cd.at[src], r_cd.at[src], column(partner))

    def onward(act, src, step):
        if step >= 0:

            @pl.when(chip < chips - 1)
            def _():
                act(src, 1)

        if step <= 0:

            @pl.when(chip > 0)
            def _():
                act(src, 0)

    def sources(distance):
        return ((chip, 0),) if distance == 0 else ((chip - distance, distance), (chip + distance, -distance))

    def valid(src):
        return jnp.logical_and(src >= 0, src < chips)

    def each(distance, act):
        for src, step in sources(distance):
            if distance == 0:
                act(src, step)
            else:

                @pl.when(valid(src))
                def _():
                    act(src, step)

    def spread_diag(src, step):
        own = step == 0
        if not own:
            z_diag(src, 0, False).wait_recv()
        onward(lambda s, way: z_diag(s, way, own).start(), src, step)
        for d in peers:
            x_diag(src, d, own).start()

    def spread_tile(src, step):
        if step != 0:
            z_tile(src, 0).wait_recv()
        onward(lambda s, way: z_tile(s, way).start(), src, step)
        c_tile(src, panel(src)).start()

    def complete_diag(src, step):
        for d in peers:
            x_arrived(src, d).wait_recv()
        c_diag(src, panel(src)).start()

    def add(src, step):
        accumulate(total, pbuf.at[panel(src)], dbuf.at[panel(src)], False)
        other = 2 * src + 1 - core
        c_tile(src, other).wait_recv()
        c_diag(src, other).wait_recv()
        accumulate(total, pbuf.at[other], dbuf.at[other], False)

    def finish(src, step):
        onward(lambda s, way: z_diag(s, way, step == 0).wait_send(), src, step)
        onward(lambda s, way: z_tile(s, way).wait_send(), src, step)
        for d in peers:
            x_diag(src, d, step == 0).wait_send()
        c_tile(src, panel(src)).wait_send()
        c_diag(src, panel(src)).wait_send()

    for d in peers:
        send(diag_right, full.at[part(row)], s_full.at[d - 1], r_full.at[d - 1], peer(d)).start()
    each(0, spread_diag)
    dbuf[me, part(row), :] = diag_left[...]
    full[part(row), :] = diag_right[...]
    for d in peers:
        source = full.at[part(lax.rem(row + rows - d, rows))]
        send(source, source, s_full.at[d - 1], r_full.at[d - 1], peer(d)).wait_recv()
    coupling = dot(tile_right[...], full[...], TN, HIGH) * weight[...]
    pbuf[me] = dot(tile_left[...], coupling, NN, HIGH)
    each(0, spread_tile)
    accumulate(total, old_left, old_right, True)
    each(0, complete_diag)
    for distance in range(1, chips):
        each(distance, spread_diag)
        each(distance, spread_tile)
        each(distance - 1, add)
        each(distance, complete_diag)
    each(chips - 1, add)
    split_into(total.at[0], high, low, 0)
    split_into(total.at[1], high, low, 1)
    for d in peers:
        send(diag_right, full.at[part(row)], s_full.at[d - 1], r_full.at[d - 1], peer(d)).wait_send()
    for distance in range(chips):
        each(distance, finish)


def local_kernel(high, low, start_ref, left_ref, right_ref, block):
    block[...] = start_ref[...]
    iterate(high, low, block, left_ref, right_ref)


def gathered(mesh_shape, tile_left, tile_right, diag_left, diag_right, weight, old_left, old_right):
    rows, past = mesh_shape["rows"], mesh_shape["past"]
    order, width = tile_left.shape
    vmem = pl.BlockSpec(memory_space=pltpu.VMEM)
    shape = jax.ShapeDtypeStruct((2, order, order), BF16)
    dma = pltpu.SemaphoreType.DMA
    chips = past // 2
    return pl.pallas_call(
        functools.partial(gather_kernel, rows, past),
        out_shape=(shape, shape),
        in_specs=[vmem] * 7,
        out_specs=(vmem, vmem),
        scratch_shapes=[
            pltpu.VMEM((past, order, width), F32),
            pltpu.VMEM((past, order, width), F32),
            pltpu.VMEM((order, width), F32),
            pltpu.VMEM((2, order, order), F32),
            dma((rows - 1,)), dma((rows - 1,)),
            dma((chips, 2)), dma((chips,)),
            dma((chips, 2)), dma((chips,)),
            dma((chips, rows - 1)), dma((chips, rows - 1)),
            dma((chips,)), dma((chips,)),
            dma((chips,)), dma((chips,)),
        ],
        compiler_params=pltpu.CompilerParams(
            collective_id=0, has_side_effects=True, vmem_limit_bytes=56 * 2**20
        ),
    )(tile_left, tile_right, diag_left, diag_right, weight, old_left, old_right)


def summed(tile_left, tile_right, diag_left, diag_right, weight, old_left, old_right):
    diag_left = lax.all_gather(diag_left, "rows", axis=0, tiled=True)
    diag_right = lax.all_gather(diag_right, "rows", axis=0, tiled=True)
    coupling = jnp.dot(tile_right.T, diag_right, precision=HIGH) * weight[0, 0]
    middle = jnp.dot(tile_left, coupling, precision=HIGH)
    past = lax.psum(jnp.dot(middle, diag_left.T, precision=HIGH), "past")
    total = jnp.dot(old_left, old_right.T, precision=HIGH) - past
    return halves(jnp.stack([total, total.T]))


def shards(mesh_shape, tile_left, tile_right, diag_left, diag_right, present, old_left, old_right, start):
    order, width = start.shape[1:]
    past = mesh_shape["past"]
    weight = jnp.broadcast_to(present.astype(F32), (1, width))
    terms = (tile_left[0, 0], tile_right[0, 0], diag_left[0], diag_right[0], weight, old_left[0], old_right[0])
    if past % 2 == 0 and mesh_shape["rows"] > 1 and 8 * past * order * width <= 16 * 2**20:
        high, low = gathered(mesh_shape, *terms)
    else:
        high, low = summed(*terms)
    shape = jax.ShapeDtypeStruct((order, width), F32)
    vmem = pl.BlockSpec(memory_space=pltpu.VMEM)
    left, right = pl.pallas_call(
        local_kernel,
        out_shape=(shape, shape),
        in_specs=[vmem] * 3,
        out_specs=(vmem, vmem),
        scratch_shapes=[pltpu.VMEM((order, width), F32)],
        compiler_params=pltpu.CompilerParams(vmem_limit_bytes=48 * 2**20),
    )(high, low, start[0])
    return left[None], right[None]


def solution(mesh):
    placed = (
        P("rows", "past", None, None),
        P("rows", "past", None, None),
        P("past", "rows", None),
        P("past", "rows", None),
        P("rows", "past"),
        P("rows", None, None),
        P("rows", None, None),
        P("rows", None, None),
    )
    return jax.shard_map(
        functools.partial(shards, dict(mesh.shape)),
        mesh=mesh,
        in_specs=placed,
        out_specs=(P("rows", None, None), P("rows", None, None)),
        check_vma=False,
    )
```

profile of v0, /device:TPU:4, one launch (start us, length us, event | category | flops | bytes accessed | tf_op | source)
XLA Modules:
  0.0 182.0 jit_solution(3734107810617262009)
XLA Ops:
  1.3 0.5 broadcast_in_dim.14.weight
  1.8 75.5 %shard_map.95 = (bf16[2,1024,1024]{2,1,0:T(8,128)(2,1)}, bf16[2,1024,1024]{2,1,0:T(8,128)(2,1)}) custom-call(f32[1024,128]{1,0:T(8,128)} %bitcast.11, f32[1024,128]{1,0:T(8,128)} %bitcast.12, f32[256,128]{1,0:T(8,128)} %bitcast.15, f32[256,128]{1,0:T(8,128)} %bitcast.16, f32[1,128]{1,0:T(1,128)} %broadcast_in_dim.14.weight, f32[1024,128]{1,0:T(8,128)} %bitcast.13, ...), custom_call_target="tpu_custom_call" | custom-call | tf_op jit(solution)/shard_map/pallas_call | solution.py:306
  77.3 0.0 copy-start
  77.3 2.2 %copy-done = bf16[2,1024,1024]{2,1,0:T(8,128)(2,1)S(1)} copy-done((bf16[2,1024,1024]{2,1,0:T(8,128)(2,1)S(1)}, bf16[2,1024,1024]{2,1,0:T(8,128)(2,1)}, u32[]{:S(2)}) %copy-start) | copy-done | bytes 4194328
  79.5 0.0 copy-start.1
  79.5 1.0 copy-done.1
  80.5 101.4 %shard_map.96 = (f32[1024,128]{1,0:T(8,128)}, f32[1024,128]{1,0:T(8,128)}) custom-call(bf16[2,1024,1024]{2,1,0:T(8,128)(2,1)S(1)} %copy-done, bf16[2,1024,1024]{2,1,0:T(8,128)(2,1)} %get-tuple-element.7.low, f32[1024,128]{1,0:T(8,128)S(1)} %bitcast.10), custom_call_target="tpu_custom_call" | custom-call | tf_op jit(solution)/shard_map/pallas_call | solution.py:350
Async XLA Ops:
  77.3 2.2 %copy-start = (bf16[2,1024,1024]{2,1,0:T(8,128)(2,1)S(1)}, bf16[2,1024,1024]{2,1,0:T(8,128)(2,1)}, u32[]{:S(2)}) copy-start(bf16[2,1024,1024]{2,1,0:T(8,128)(2,1)} %get-tuple-element.6.high) | copy-start | bytes 12582916
  79.5 1.0 copy-start.1
where the time goes:
time: 182 us
  Pallas kernels  177 us (97%)
  local copies, waits for them, and re-layouts  3.74 us (2%)
    pallas_call x1, Pallas kernels, shards(): pl.pallas_call(local_kernel, out_shape=(shape, shape), in_specs=[vmem] *...  101 us
    pallas_call x1, Pallas kernels, gathered(): pl.pallas_call(functools.partial(gather_kernel, rows, past), out_shape=(s...  75.5 us

commit v1 on v0

--- a/solution.py
+++ b/solution.py
@@ -35,29 +35,62 @@
 
 def lower_inverse(gram):
     size = gram.shape[0]
-    rows = [gram[8 * b : 8 * b + 8] for b in range(size // 8)]
-    lane = lax.broadcasted_iota(jnp.int32, (8, size), 1)
-    sub = lax.broadcasted_iota(jnp.int32, (8, size), 0)
-    for k in range(size):
-        own, s = divmod(k, 8)
-        pivot_row = rows[own][s : s + 1]
-        inverse = 1.0 / pivot_row[:, k : k + 1]
-        at_pivot = lane == k
-        scaled = jnp.broadcast_to(
-            jnp.where(lane[:1] == k, 1.0, pivot_row) * inverse, (8, size)
-        )
-        for b in range(own, size // 8):
-            if b == own and s == 7:
-                continue
-            factor = jnp.broadcast_to(rows[b][:, k : k + 1], (8, size))
-            fresh = jnp.where(at_pivot, 0.0, rows[b]) - factor * scaled
-            rows[b] = jnp.where(sub > s, fresh, rows[b]) if b == own else fresh
+    step = 8
+    lane = lax.broadcasted_iota(jnp.int32, (step, size), 1)
+    sub = lax.broadcasted_iota(jnp.int32, (step, size), 0)
+    rows = [gram[step * b : step * (b + 1)] for b in range(size // step)]
     out = []
-    for b in range(size // 8):
-        diagonal = lane == sub + 8 * b
-        pivot = jnp.sum(jnp.where(diagonal, rows[b], 0.0), axis=1, keepdims=True)
-        unit = jnp.where(lane < sub + 8 * b, rows[b], jnp.where(diagonal, 1.0, 0.0))
-        out.append(unit * lax.rsqrt(pivot))
+
+    def all_rows(value, i):
+        return jnp.broadcast_to(value[i : i + 1], (step, size))
+
+    def all_lanes(value, k):
+        return jnp.broadcast_to(value[:, k : k + 1], (step, size))
+
+    for b in range(size // step):
+        base = step * b
+        own = rows[b]
+        inside = jnp.logical_and(lane >= base, lane < base + step)
+        start = jnp.where(inside, jnp.where(lane - base == sub, 1.0, 0.0), own)
+        begun = [all_rows(start, k) for k in range(step)]
+        columns = [all_lanes(own, base + k) for k in range(step)]
+        a = {(i, k): all_rows(columns[k], i) for k in range(step) for i in range(k, step)}
+        n = {}
+        for k in range(step):
+            root = lax.rsqrt(a[k, k])
+            for j in range(k):
+                n[k, j] = n[k, j] * root
+            n[k, k] = root
+            scaled = {i: a[i, k] * root for i in range(k + 1, step)}
+            for i in range(k + 1, step):
+                for j in range(k + 1, i + 1):
+                    a[i, j] = a[i, j] - scaled[i] * scaled[j]
+                for j in range(k):
+                    n[i, j] = n[i, j] - scaled[i] * n[k, j]
+                n[i, k] = -scaled[i] * root
+        done = []
+        for m in range(step):
+            value = n[m, 0] * begun[0]
+            for j in range(1, m + 1):
+                value = value + n[m, j] * begun[j]
+            done.append(value)
+        own = done[0]
+        for m in range(1, step):
+            own = jnp.where(sub == m, done[m], own)
+        out.append(jnp.where(lane < base + step, own, 0.0))
+        if b + 1 == size // step:
+            break
+        solved = []
+        for k in range(step):
+            value = n[k, k] * done[k]
+            for m in range(k + 1, step):
+                value = value + n[m, k] * done[m]
+            solved.append(value)
+        for t in range(b + 1, size // step):
+            value = all_lanes(rows[t], base) * solved[0]
+            for k in range(1, step):
+                value = value + all_lanes(rows[t], base + k) * solved[k]
+            rows[t] = jnp.where(inside, 0.0, rows[t]) - value
     return jnp.concatenate(out, 0)
 
 
@@ -98,7 +131,7 @@
         apply_matrix(high_ref, low_ref, lax.rem(t, 2), block_ref[...], right_ref)
         value = right_ref[...]
         inverse = lower_inverse(dot(value, value, TN, HIGH))
-        block_ref[...] = dot(value, inverse, NT, HIGH)
+        block_ref[...] = wide_nt(value, inverse)
         return carry
 
     lax.fori_loop(0, 2 * ITERS + 1, step, 0)

time: 182 us -> 140 us (0.77)
  Pallas kernels: 177 us -> 134 us
    pallas_call x1, Pallas kernels: 101 us -> 58.8 us  [shards(): pl.pallas_call(local_kernel, out_shape=(shape, shape), in_specs=[vmem] *...]
where the time goes in v1:
time: 140 us; the launch traced here: 139 us
  Pallas kernels  134 us (96%)
  local copies, waits for them, and re-layouts  3.74 us (3%)
    pallas_call x1, Pallas kernels, gathered(): pl.pallas_call(functools.partial(gather_kernel, rows, past), out_shape=(s...  75.5 us
    pallas_call x1, Pallas kernels, shards(): pl.pallas_call(local_kernel, out_shape=(shape, shape), in_specs=[vmem] *...  58.8 us
    unnamed x4, local copies, waits for them, and re-layouts  3.22 us

profile of v1, /device:TPU:4, one launch (start us, length us, event | category | flops | bytes accessed | tf_op | source)
XLA Modules:
  0.0 139.3 jit_solution(37104640960734743)
XLA Ops:
  1.3 0.5 broadcast_in_dim.14.weight
  1.8 75.5 %shard_map.95 = (bf16[2,1024,1024]{2,1,0:T(8,128)(2,1)}, bf16[2,1024,1024]{2,1,0:T(8,128)(2,1)}) custom-call(f32[1024,128]{1,0:T(8,128)} %bitcast.11, f32[1024,128]{1,0:T(8,128)} %bitcast.12, f32[256,128]{1,0:T(8,128)} %bitcast.15, f32[256,128]{1,0:T(8,128)} %bitcast.16, f32[1,128]{1,0:T(1,128)} %broadcast_in_dim.14.weight, f32[1024,128]{1,0:T(8,128)} %bitcast.13, ...), custom_call_target="tpu_custom_call" | custom-call | tf_op jit(solution)/shard_map/pallas_call | solution.py:339
  77.3 0.0 copy-start
  77.3 2.2 %copy-done = bf16[2,1024,1024]{2,1,0:T(8,128)(2,1)S(1)} copy-done((bf16[2,1024,1024]{2,1,0:T(8,128)(2,1)S(1)}, bf16[2,1024,1024]{2,1,0:T(8,128)(2,1)}, u32[]{:S(2)}) %copy-start) | copy-done | bytes 4194328
  79.5 0.0 copy-start.1
  79.5 1.0 copy-done.1
  80.5 58.8 %shard_map.96 = (f32[1024,128]{1,0:T(8,128)}, f32[1024,128]{1,0:T(8,128)}) custom-call(bf16[2,1024,1024]{2,1,0:T(8,128)(2,1)S(1)} %copy-done, bf16[2,1024,1024]{2,1,0:T(8,128)(2,1)} %get-tuple-element.7.low, f32[1024,128]{1,0:T(8,128)S(1)} %bitcast.10), custom_call_target="tpu_custom_call" | custom-call | tf_op jit(solution)/shard_map/pallas_call | solution.py:383
Async XLA Ops:
  77.3 2.2 %copy-start = (bf16[2,1024,1024]{2,1,0:T(8,128)(2,1)S(1)}, bf16[2,1024,1024]{2,1,0:T(8,128)(2,1)}, u32[]{:S(2)}) copy-start(bf16[2,1024,1024]{2,1,0:T(8,128)(2,1)} %get-tuple-element.6.high) | copy-start | bytes 12582916
  79.5 1.0 copy-start.1
